TPU v7x, 32 devices: a whole 2x2x4 slice. The times are simulated.
32 devices in a mesh: ctx: 16 (over z, y, x), head: 2 (over core).
Axes of the slice: x: 2, y: 2, z: 4, core: 2. Of those that a mesh axis runs over, the one named last changes fastest.
Arguments:
- query: bfloat16 [4096, 8192], P(('ctx', 'head')), may hold values from -20 to 20
- key: bfloat16 [4096, 1024], P(('ctx', 'head')), may hold values from -6 to 6
- value: bfloat16 [4096, 1024], P(('ctx', 'head')), may hold values from -6 to 6
- doc_lengths: int32 [4], replicated, may hold values from 256 to 2048, as said below
- block_place: int32 [256], replicated, may hold values from 0 to 255, as said below
Outputs:
- attended: bfloat16 [4096, 8192], P('ctx', 'head')
Inputs may be any that keep to these rules, and one draw needn't show every extreme that they name: `doc_lengths`: 4 lengths that sum to 4096; the longest is exactly 2048 and the shortest exactly 256. `block_place`: A permutation of the blocks. The 8 blocks of one loading device (one index of ctx+head, ctx slowest) go to distinct context shards; context shard s holds packed blocks s * 16 to (s + 1) * 16 - 1.
All inputs are finite; a program needn't handle non-finite values.
Results may differ from a plain program's by a relative error of at most 0.0028.
Values may be sent and summed in bfloat16 or wider, within the bound.
No kernel may reach another device: no remote copies, remote signals or barrier semaphores. Data moves between devices by JAX's collectives and lax.ppermute only.
A program may use at most 192 MiB of HBM per device.

v0:
```python
import functools

import jax
import jax.numpy as jnp
import numpy as np
from jax import lax
from jax.experimental import pallas as pl
from jax.experimental.pallas import tpu as pltpu
from jax.sharding import PartitionSpec as P

HD = 128
SPAN = 8
MASKED = -1e30
EXP2_SCALE = float(HD ** (-0.5) * np.log2(np.e))
VMEM_LIMIT = 60 * 1024 * 1024
ANY = pl.BlockSpec(memory_space=pl.ANY)


def pack_query_kernel(chunks, place_ref, loader_ref, query, *refs):
    outs, sems = refs[:chunks], refs[chunks]
    per_loader = query.shape[0]
    width = outs[0].shape[2]
    copies = []
    for chunk in range(chunks):
        for j in range(per_loader):
            target = place_ref[loader_ref[0] * per_loader + j] // loader_ref[1]
            for side in range(2):
                copy = pltpu.make_async_copy(
                    query.at[j, :, pl.ds((side * chunks + chunk) * width, width)],
                    outs[chunk].at[target * 2 + side],
                    sems.at[len(copies)],
                )
                copy.start()
                copies.append(copy)
    for copy in copies:
        copy.wait()


def pack_pair_kernel(place_ref, loader_ref, key, value, out, sems):
    per_loader = key.shape[0]
    half = key.shape[2] // 2
    copies = []
    for j in range(per_loader):
        target = place_ref[loader_ref[0] * per_loader + j] // loader_ref[1]
        for side in range(2):
            for at, source in enumerate((key, value)):
                copy = pltpu.make_async_copy(
                    source.at[j, :, pl.ds(side * half, half)],
                    out.at[target * 2 + side, :, pl.ds(at * half, half)],
                    sems.at[len(copies)],
                )
                copy.start()
                copies.append(copy)
    for copy in copies:
        copy.wait()


def whole(shape):
    return pl.BlockSpec(shape, lambda i, *_: (0,) * len(shape))


def call(kernel, scalars, arrays, in_specs, outs, out_specs, scratch, name, **more):
    return pl.pallas_call(
        kernel,
        out_shape=outs,
        grid_spec=pltpu.PrefetchScalarGridSpec(
            num_scalar_prefetch=len(scalars),
            grid=(1,),
            in_specs=in_specs,
            out_specs=out_specs,
            scratch_shapes=scratch,
        ),
        compiler_params=pltpu.CompilerParams(vmem_limit_bytes=VMEM_LIMIT),
        name=name,
        **more,
    )(*scalars, *arrays)


def moved(count):
    return pl.CostEstimate(flops=0, transcendentals=0, bytes_accessed=count)


def pick_for_targets(blocks, block_place, loader, shard_blocks, shards):
    per_loader = blocks.shape[0]
    assigned = lax.dynamic_slice_in_dim(block_place, loader * per_loader, per_loader)
    matched = (assigned // shard_blocks)[None, :] == jnp.arange(shards, dtype=jnp.int32)[:, None]
    return jnp.take(blocks, jnp.argmax(matched, axis=1), axis=0)


def pack_query(query, block_place, loader, shard_blocks, slots, chunks):
    rows, columns = query.shape
    per_loader = block_place.shape[0] // slots
    block_rows = rows // per_loader
    width = columns // 2 // chunks
    blocks = query.reshape(per_loader, block_rows, columns)
    if block_rows % 16:
        picked = pick_for_targets(blocks, block_place, loader, shard_blocks, slots // 2)
        picked = picked.reshape(slots // 2, block_rows, 2, chunks, width)
        return [
            jnp.swapaxes(picked[:, :, :, chunk], 1, 2).reshape(slots, block_rows, width)
            for chunk in range(chunks)
        ]
    return call(
        functools.partial(pack_query_kernel, chunks),
        (block_place, jnp.stack([loader, jnp.int32(shard_blocks)])),
        (blocks,),
        [whole(blocks.shape)],
        [jax.ShapeDtypeStruct((slots, block_rows, width), query.dtype)] * chunks,
        [ANY] * chunks,
        [pltpu.SemaphoreType.DMA((2 * chunks * per_loader,))],
        "pack_query",
        cost_estimate=moved(4 * rows * columns),
    )


def pack_pair(key, value, block_place, loader, shard_blocks, slots):
    rows, columns = key.shape
    per_loader = block_place.shape[0] // slots
    block_rows = rows // per_loader
    keys, values = (x.reshape(per_loader, block_rows, columns) for x in (key, value))
    if block_rows % 16:
        both = jnp.stack([keys, values], axis=2).reshape(
            per_loader, block_rows, 2, 2, columns // 2
        )
        picked = pick_for_targets(both, block_place, loader, shard_blocks, slots // 2)
        return jnp.transpose(picked, (0, 3, 1, 2, 4)).reshape(slots, block_rows, columns)
    return call(
        pack_pair_kernel,
        (block_place, jnp.stack([loader, jnp.int32(shard_blocks)])),
        (keys, values),
        [whole(keys.shape)] * 2,
        jax.ShapeDtypeStruct((slots, block_rows, columns), key.dtype),
        ANY,
        [pltpu.SemaphoreType.DMA((4 * per_loader,))],
        "pack_pair",
        cost_estimate=moved(8 * rows * columns),
    )


def pick_kernel(rows_ref, blocks, out, sem):
    copies = []
    for i in range(out.shape[0]):
        copy = pltpu.make_async_copy(blocks.at[rows_ref[i]], out.at[i], sem.at[i])
        copy.start()
        copies.append(copy)
    for copy in copies:
        copy.wait()


def pick_unit(arrived, sources):
    count = sources.shape[0]
    block_rows, width = arrived.shape[1:]
    if block_rows % 16:
        unit = jnp.take(arrived, sources, axis=0)
    else:
        shape = (count, block_rows, width)
        unit = call(
            pick_kernel,
            (sources,),
            (arrived,),
            [ANY],
            jax.ShapeDtypeStruct(shape, arrived.dtype),
            whole(shape),
            [pltpu.SemaphoreType.DMA((count,))],
            "pick_unit",
            cost_estimate=moved(4 * count * block_rows * width),
        )
    return unit.reshape(count * block_rows, width)


def spread(unit, shard):
    shards = lax.axis_size("ctx")
    plane = SPAN // 2
    place = shard % plane

    def forward(x):
        return lax.ppermute(x, "ctx", [(s, s + plane) for s in range(shards - plane)])

    before = forward(unit)
    oldest = forward(before)
    units = [unit, before, oldest]
    places = [jnp.int32(SPAN), jnp.int32(plane), jnp.int32(0)]
    sent = {}
    for mask in range(1, plane):
        partner = place ^ mask
        lower = place < partner
        bit = mask.bit_length()
        if bit not in sent:
            sent[bit] = jnp.where(lower, unit, oldest)
        route = [(s, s ^ mask) for s in range(shards)]
        units.append(lax.ppermute(before, "ctx", route))
        places.append(plane - place + partner)
        units.append(lax.ppermute(sent[bit], "ctx", route))
        places.append(jnp.where(lower, 0, SPAN) - place + partner)
    return units, jnp.stack(places).astype(jnp.int32)


def attend_kernel(chunk, docs, heads, slot_ref, lengths_ref, shard_ref, places_ref, *refs):
    arrived, units = refs[0], refs[1 : SPAN + 2]
    out, queries, keys, values, maxes, sums, sem, key_sem = refs[-8:]
    blocks, block_rows, width = queries.shape
    rows = blocks * block_rows
    tiles, tile = keys.shape[:2]
    copies = []
    for i in range(blocks):
        copy = pltpu.make_async_copy(arrived.at[slot_ref[i]], queries.at[i], sem.at[i])
        copy.start()
        copies.append(copy)
    half = units[0].shape[1] // 2

    def fetch(unit, at, which):
        target = (keys, values)[which]
        columns = pl.ds(which * half + chunk * HD, HD)
        return pltpu.make_async_copy(unit.at[:, columns], target.at[at], key_sem.at[which, at])

    for unit, ref in enumerate(units):
        for which in range(2):
            fetch(ref, places_ref[unit], which).start()
    first_row = shard_ref[0] * rows
    query_rows = first_row + lax.broadcasted_iota(jnp.int32, (1, rows), 1)
    starts = jnp.zeros((1, rows), jnp.int32)
    first_start = jnp.int32(0)
    end = jnp.int32(0)
    for d in range(docs):
        length = lengths_ref[d]
        end = end + length
        starts = starts + jnp.where(query_rows >= end, length, 0)
        first_start = first_start + jnp.where(first_row >= end, length, 0)
    window_start = first_row + rows - tiles * tile
    diagonal = tiles - 1
    first_tile = (first_start - window_start) // tile
    for h in range(heads):
        maxes[h] = jnp.full((1, rows), MASKED, jnp.float32)
        sums[h] = jnp.zeros(sums.shape[1:], jnp.float32)
    for copy in copies:
        copy.wait()

    def landed(index):
        for which in range(2):
            fetch(units[0], index, which).wait()

    def unused(index, carry):
        landed(index)
        return carry

    lax.fori_loop(0, first_tile, unused, 0)

    def step(index, masked, last):
        landed(index)
        tile_keys = keys[index]
        tile_values = values[index]
        extended = jnp.concatenate([tile_values, jnp.ones((tile, HD), tile_values.dtype)], axis=1)
        turned = extended.T[: HD + 16]
        if masked:
            key_rows = window_start + index * tile + lax.broadcasted_iota(jnp.int32, (tile, rows), 0)
            visible = (key_rows >= starts) & (key_rows <= query_rows)
        if last:
            later = starts >= first_row

        def score(h):
            query = queries[:, :, h * HD : (h + 1) * HD].reshape(rows, HD)
            return lax.dot_general(
                tile_keys, query, (((1,), (1,)), ((), ())), preferred_element_type=jnp.float32
            )

        ahead = score(0)
        for h in range(heads):
            scores = ahead
            if h + 1 < heads:
                ahead = score(h + 1)
            if masked:
                scores = jnp.where(visible, scores, MASKED)
            old = maxes[h]
            if last:
                old = jnp.where(later, MASKED, old)
            new = jnp.maximum(old, jnp.max(scores, axis=0, keepdims=True))
            scaled = new * EXP2_SCALE
            weights = jnp.exp2(scores * EXP2_SCALE - scaled).astype(jnp.bfloat16)
            factor = jnp.exp2(old * EXP2_SCALE - scaled)
            product = jnp.dot(turned, weights, preferred_element_type=jnp.float32)
            total = sums[h] * factor + product
            if last:
                result = total[:HD] / total[HD : HD + 1]
                out[:, h * HD : (h + 1) * HD] = result.T.astype(out.dtype)
            else:
                maxes[h] = new
                sums[h] = total

    @pl.when(first_tile < diagonal)
    def _():
        step(first_tile, True, False)

    def middle(index, carry):
        step(index, False, False)
        return carry

    lax.fori_loop(first_tile + 1, diagonal, middle, 0)
    step(diagonal, True, True)


def attend(arrived, units, places, slots, doc_lengths, shard, chunk, chunks, result):
    block_rows, width = arrived.shape[1:]
    shard_rows = units[0].shape[0]
    blocks = shard_rows // block_rows
    if block_rows % 16:
        arrived = jnp.take(arrived, slots, axis=0).reshape(shard_rows // 16, 16, width)
        block_rows, blocks = 16, shard_rows // 16
        slots = jnp.arange(blocks, dtype=jnp.int32)
    heads = width // HD
    tiles = len(units)
    aliased = [] if result is None else [result]
    scalars = (slots, doc_lengths, shard, places)
    arrays = (arrived, *units, *aliased)
    return call(
        functools.partial(attend_kernel, chunk, doc_lengths.shape[0], heads),
        scalars,
        arrays,
        [ANY] * len(arrays),
        jax.ShapeDtypeStruct((shard_rows, chunks * width), arrived.dtype),
        pl.BlockSpec((shard_rows, width), lambda i, *_: (0, chunk)),
        [
            pltpu.VMEM((blocks, block_rows, width), arrived.dtype),
            pltpu.VMEM((tiles, shard_rows, HD), arrived.dtype),
            pltpu.VMEM((tiles, shard_rows, HD), arrived.dtype),
            pltpu.VMEM((heads, 1, shard_rows), jnp.float32),
            pltpu.VMEM((heads, HD + 16, shard_rows), jnp.float32),
            pltpu.SemaphoreType.DMA((blocks,)),
            pltpu.SemaphoreType.DMA((2, tiles)),
        ],
        f"attend{chunk}",
        input_output_aliases={len(scalars) + len(arrays) - 1: 0} if aliased else {},
        cost_estimate=pl.CostEstimate(
            flops=4 * shard_rows * shard_rows * tiles * width,
            transcendentals=shard_rows * shard_rows * tiles * heads,
            bytes_accessed=4 * shard_rows * (width + tiles * HD),
        ),
    )


def body(query, key, value, doc_lengths, block_place):
    ctx_count = lax.axis_size("ctx")
    head_count = lax.axis_size("head")
    loaded_rows = query.shape[0]
    shard_rows = loaded_rows * head_count
    block_rows = shard_rows // ctx_count
    per_loader = loaded_rows // block_rows
    shard_blocks = shard_rows // block_rows
    shard = lax.axis_index("ctx").astype(jnp.int32)
    group = lax.axis_index("head").astype(jnp.int32)
    loader = shard * head_count + group
    slots = ctx_count * head_count
    chunks = key.shape[1] // head_count // HD
    def exchange(sends):
        return lax.all_to_all(sends, ("ctx", "head"), split_axis=0, concat_axis=0, tiled=True)

    pair = exchange(pack_pair(key, value, block_place, loader, shard_blocks, slots))
    sends = list(pack_query(query, block_place, loader, shard_blocks, slots, chunks))
    wanted = shard * shard_blocks + jnp.arange(shard_blocks, dtype=jnp.int32)
    places = jnp.arange(block_place.shape[0], dtype=jnp.int32)
    inverse = jnp.sum(jnp.where(wanted[:, None] == block_place[None, :], places[None, :], 0), axis=1)
    sources = inverse // per_loader
    unit = pick_unit(pair, sources)
    sends[0], unit = lax.optimization_barrier((sends[0], unit))
    units, unit_places = spread(unit, shard)
    for chunk, stage in ((1, 1), (2, 2), (3, 2)):
        if chunk < chunks:
            sends[chunk], units[stage] = lax.optimization_barrier((sends[chunk], units[stage]))
    arrived = [exchange(send) for send in sends]
    result = None
    for chunk in range(chunks):
        result = attend(
            arrived[chunk],
            units,
            unit_places,
            sources,
            doc_lengths,
            shard[None],
            chunk,
            chunks,
            result,
        )
    return result


def solution(mesh):
    placed = (
        P(("ctx", "head"), None),
        P(("ctx", "head"), None),
        P(("ctx", "head"), None),
        P(),
        P(),
    )
    return jax.shard_map(
        body, mesh=mesh, in_specs=placed, out_specs=P("ctx", "head"), check_vma=False
    )
```

profile of v0, /device:TPU:30, one launch (start us, length us, event | category | flops | bytes accessed | tf_op | source)
XLA Modules:
  0.0 267.7 jit_solution(14904597321791053465)
XLA Ops:
  0.7 2.8 %pack_pair.1 = bf16[32,16,1024]{2,1,0:T(8,128)(2,1)} custom-call(s32[256]{0:T(256)} %place_ref.3, s32[2]{0:T(128)} %pad_add_fusion.loader_ref, bf16[8,16,1024]{2,1,0:T(8,128)(2,1)} %bitcast.19, bf16[8,16,1024]{2,1,0:T(8,128)(2,1)} %bitcast.20), custom_call_target="tpu_custom_call" | custom-call | bytes 1048576 | tf_op jit(solution)/shard_map/pack_pair/pallas_call | solution.py:63
  3.5 5.8 %all-to-all-start = ((bf16[32,16,1024]{2,1,0:T(8,128)(2,1)}), bf16[32,16,1024]{2,1,0:T(8,128)(2,1)S(1)}, u32[]{:S(2)}, u32[]{:S(2)}) async-start(bf16[32,16,1024]{2,1,0:T(8,128)(2,1)} %pack_pair.1), calls=%async_computation | async-start | bytes 2097152 | tf_op jit(solution)/shard_map/all_to_all | solution.py:354
  9.3 4.1 %pack_query.1 = (bf16[32,16,1024]{2,1,0:T(8,128)(2,1)}, bf16[32,16,1024]{2,1,0:T(8,128)(2,1)}, bf16[32,16,1024]{2,1,0:T(8,128)(2,1)}, bf16[32,16,1024]{2,1,0:T(8,128)(2,1)}) custom-call(s32[256]{0:T(256)} %place_ref.3, s32[2]{0:T(128)} %pad_add_fusion.loader_ref, bf16[8,16,8192]{2,1,0:T(8,128)(2,1)} %bitcast.18), custom_call_target="tpu_custom_call" | custom-call | bytes 4194304 | tf_op jit(solution)/shard_map/pack_query/pallas_call | solution.py:63
  14.3 19.1 %all-to-all-done.blocks = bf16[32,16,1024]{2,1,0:T(8,128)(2,1)S(1)} async-done(((bf16[32,16,1024]{2,1,0:T(8,128)(2,1)}), bf16[32,16,1024]{2,1,0:T(8,128)(2,1)S(1)}, u32[]{:S(2)}, u32[]{:S(2)}) %all-to-all-start) | async-done | bytes 1048608 | tf_op jit(solution)/shard_map/all_to_all | solution.py:354
  34.3 2.6 pick_unit.1
  37.0 5.8 %all-to-all-start.4 = ((bf16[32,16,1024]{2,1,0:T(8,128)(2,1)}), bf16[32,16,1024]{2,1,0:T(8,128)(2,1)S(1)}, u32[]{:S(2)}, u32[]{:S(2)}) async-start(bf16[32,16,1024]{2,1,0:T(8,128)(2,1)} %get-tuple-element.28), calls=%async_computation.4 | async-start | bytes 2097152 | tf_op jit(solution)/shard_map/all_to_all | solution.py:354
  44.1 28.4 %collective-permute-done.refs_2_ = bf16[256,1024]{1,0:T(8,128)(2,1)S(1)} collective-permute-done((bf16[256,1024]{1,0:T(8,128)(2,1)S(1)}, bf16[256,1024]{1,0:T(8,128)(2,1)S(1)}, u32[]{:S(2)}, u32[]{:S(2)}) %collective-permute-start) | collective-permute-done | bytes 524320 | tf_op jit(solution)/shard_map/ppermute | solution.py:177
  73.5 10.6 %all-to-all-start.3 = ((bf16[32,16,1024]{2,1,0:T(8,128)(2,1)}), bf16[32,16,1024]{2,1,0:T(8,128)(2,1)S(1)}, u32[]{:S(2)}, u32[]{:S(2)}) async-start(bf16[32,16,1024]{2,1,0:T(8,128)(2,1)} %get-tuple-element.27), calls=%async_computation.3 | async-start | bytes 2097152 | tf_op jit(solution)/shard_map/all_to_all | solution.py:354
  85.4 28.4 %collective-permute-done.1.refs_3_ = bf16[256,1024]{1,0:T(8,128)(2,1)S(1)} collective-permute-done((bf16[256,1024]{1,0:T(8,128)(2,1)S(1)}, bf16[256,1024]{1,0:T(8,128)(2,1)S(1)}, u32[]{:S(2)}, u32[]{:S(2)}) %collective-permute-start.1) | collective-permute-done | bytes 524320 | tf_op jit(solution)/shard_map/ppermute | solution.py:177
  113.8 10.6 %all-to-all-start.2 = ((bf16[32,16,1024]{2,1,0:T(8,128)(2,1)}), bf16[32,16,1024]{2,1,0:T(8,128)(2,1)}, u32[]{:S(2)}, u32[]{:S(2)}) async-start(bf16[32,16,1024]{2,1,0:T(8,128)(2,1)} %get-tuple-element.26), calls=%async_computation.2 | async-start | bytes 2097152 | tf_op jit(solution)/shard_map/all_to_all | solution.py:354
  124.4 24.1 %all-to-all-done.2.refs_0_ = bf16[32,16,1024]{2,1,0:T(8,128)(2,1)} async-done(((bf16[32,16,1024]{2,1,0:T(8,128)(2,1)}), bf16[32,16,1024]{2,1,0:T(8,128)(2,1)}, u32[]{:S(2)}, u32[]{:S(2)}) %all-to-all-start.2) | async-done | bytes 1048608 | tf_op jit(solution)/shard_map/all_to_all | solution.py:354
  148.5 5.9 %all-to-all-start.1 = ((bf16[32,16,1024]{2,1,0:T(8,128)(2,1)}), bf16[32,16,1024]{2,1,0:T(8,128)(2,1)}, u32[]{:S(2)}, u32[]{:S(2)}) async-start(bf16[32,16,1024]{2,1,0:T(8,128)(2,1)} %get-tuple-element.22), calls=%async_computation.1 | async-start | bytes 2097152 | tf_op jit(solution)/shard_map/all_to_all | solution.py:354
  154.9 1.5 collective-permute-start.4
  156.4 1.5 collective-permute-start.2
  159.6 1.4 collective-permute-start.7
  161.0 18.9 %collective-permute-done.6.refs_8_ = bf16[256,1024]{1,0:T(8,128)(2,1)S(1)} collective-permute-done((bf16[256,1024]{1,0:T(8,128)(2,1)S(1)}, bf16[256,1024]{1,0:T(8,128)(2,1)S(1)}, u32[]{:S(2)}, u32[]{:S(2)}) %collective-permute-start.6) | collective-permute-done | bytes 524320 | tf_op jit(solution)/shard_map/ppermute | solution.py:191
  182.0 7.4 %collective-permute-done.4.refs_6_ = bf16[256,1024]{1,0:T(8,128)(2,1)S(1)} collective-permute-done((bf16[256,1024]{1,0:T(8,128)(2,1)S(1)}, bf16[256,1024]{1,0:T(8,128)(2,1)S(1)}, u32[]{:S(2)}, u32[]{:S(2)}) %collective-permute-start.4) | collective-permute-done | bytes 524320 | tf_op jit(solution)/shard_map/ppermute | solution.py:191
  189.4 1.7 collective-permute-done.2.refs_4_
  191.1 11.2 %collective-permute-done.3.refs_5_ = bf16[256,1024]{1,0:T(8,128)(2,1)S(1)} collective-permute-done((bf16[256,1024]{1,0:T(8,128)(2,1)}, bf16[256,1024]{1,0:T(8,128)(2,1)S(1)}, u32[]{:S(2)}, u32[]{:S(2)}) %collective-permute-start.3) | collective-permute-done | bytes 524320 | tf_op jit(solution)/shard_map/ppermute | solution.py:193
  202.3 10.9 %collective-permute-done.7.refs_9_ = bf16[256,1024]{1,0:T(8,128)(2,1)S(1)} collective-permute-done((bf16[256,1024]{1,0:T(8,128)(2,1)}, bf16[256,1024]{1,0:T(8,128)(2,1)S(1)}, u32[]{:S(2)}, u32[]{:S(2)}) %collective-permute-start.7) | collective-permute-done | bytes 524320 | tf_op jit(solution)/shard_map/ppermute | solution.py:193
  214.1 13.3 %attend0.1.refs_10_ = bf16[256,4096]{1,0:T(8,128)(2,1)} custom-call(s32[16]{0:T(128)} %and_select_fusion.rows_ref.slot_ref, s32[4]{0:T(128)} %lengths_ref.7, s32[1]{0:T(128)} %bitcast.shard_ref, s32[9]{0:T(128)} %stack.35.places_ref, bf16[32,16,1024]{2,1,0:T(8,128)(2,1)} %copy-done.10, bf16[256,1024]{1,0:T(8,128)(2,1)} %bitcast.12, ...), custom_call_target="tpu_custom_call" | custom-call | flops 2415919104 | bytes 2228224 | tf_op jit(solution)/shard_map/attend0/pallas_call | solution.py:63
  227.4 13.3 %attend1.1.refs_10_ = bf16[256,4096]{1,0:T(8,128)(2,1)} custom-call(s32[16]{0:T(128)} %and_select_fusion.rows_ref.slot_ref, s32[4]{0:T(128)} %lengths_ref.7, s32[1]{0:T(128)} %bitcast.shard_ref, s32[9]{0:T(128)} %stack.35.places_ref, bf16[32,16,1024]{2,1,0:T(8,128)(2,1)} %copy-done.9, bf16[256,1024]{1,0:T(8,128)(2,1)} %bitcast.13, ...), custom_call_target="tpu_custom_call", output_to_operand_aliasing={{}: (14, {})} | custom-call | flops 2415919104 | bytes 2228224 | tf_op jit(solution)/shard_map/attend1/pallas_call | solution.py:63
  240.7 13.5 %attend2.1.refs_10_ = bf16[256,4096]{1,0:T(8,128)(2,1)} custom-call(s32[16]{0:T(128)} %and_select_fusion.rows_ref.slot_ref, s32[4]{0:T(128)} %lengths_ref.7, s32[1]{0:T(128)} %bitcast.shard_ref, s32[9]{0:T(128)} %stack.35.places_ref, bf16[32,16,1024]{2,1,0:T(8,128)(2,1)} %all-to-all-done.2.refs_0_, ...), custom_call_target="tpu_custom_call", output_to_operand_aliasing={{}: (14, {})} | custom-call | flops 2415919104 | bytes 2228224 | tf_op jit(solution)/shard_map/attend2/pallas_call | solution.py:63
  254.2 13.3 %attend3.1 = bf16[256,4096]{1,0:T(8,128)(2,1)} custom-call(s32[16]{0:T(128)} %and_select_fusion.rows_ref.slot_ref, s32[4]{0:T(128)} %lengths_ref.7, s32[1]{0:T(128)} %bitcast.shard_ref, s32[9]{0:T(128)} %stack.35.places_ref, bf16[32,16,1024]{2,1,0:T(8,128)(2,1)} %all-to-all-done.1.refs_0_, ...), custom_call_target="tpu_custom_call", output_to_operand_aliasing={{}: (14, {})} | custom-call | flops 2415919104 | bytes 2228224 | tf_op jit(solution)/shard_map/attend3/pallas_call | solution.py:63
  (39 shorter events, 11.1 us)
Async XLA Ops:
  3.5 10.0 %copy-start.11 = (s32[256]{0:T(256)S(1)}, s32[256]{0:T(256)}, u32[]{:S(2)}) copy-start(s32[256]{0:T(256)} %place_ref.3) | copy-start | bytes 3076
  3.5 29.9 %all-to-all-start = ((bf16[32,16,1024]{2,1,0:T(8,128)(2,1)}), bf16[32,16,1024]{2,1,0:T(8,128)(2,1)S(1)}, u32[]{:S(2)}, u32[]{:S(2)}) async-start(bf16[32,16,1024]{2,1,0:T(8,128)(2,1)} %pack_pair.1), calls=%async_computation | async-start | bytes 2097152 | tf_op jit(solution)/shard_map/all_to_all | solution.py:354
  33.4 1.0 copy-start.8
  37.0 5.9 %copy-start = (bf16[16,16,1024]{2,1,0:T(8,128)(2,1)S(1)}, bf16[16,16,1024]{2,1,0:T(8,128)(2,1)}, u32[]{:S(2)}) copy-start(bf16[16,16,1024]{2,1,0:T(8,128)(2,1)} %pick_unit.1) | copy-start | bytes 1572868
  37.0 35.5 %all-to-all-start.4 = ((bf16[32,16,1024]{2,1,0:T(8,128)(2,1)}), bf16[32,16,1024]{2,1,0:T(8,128)(2,1)S(1)}, u32[]{:S(2)}, u32[]{:S(2)}) async-start(bf16[32,16,1024]{2,1,0:T(8,128)(2,1)} %get-tuple-element.28), calls=%async_computation.4 | async-start | bytes 2097152 | tf_op jit(solution)/shard_map/all_to_all | solution.py:354
  42.8 29.7 %collective-permute-start = (bf16[256,1024]{1,0:T(8,128)(2,1)S(1)}, bf16[256,1024]{1,0:T(8,128)(2,1)S(1)}, u32[]{:S(2)}, u32[]{:S(2)}) collective-permute-start(bf16[256,1024]{1,0:T(8,128)(2,1)S(1)} %bitcast.16), channel_id=1, source_target_pairs={{0,8},{2,10},{4,12},{6,14},{8,16},{10,18},{12,20},{14,22},{16,24},... | collective-permute-start | bytes 1572872 | tf_op jit(solution)/shard_map/ppermute | solution.py:177
  72.5 83.9 %copy-start.2 = (bf16[256,1024]{1,0:T(8,128)(2,1)}, bf16[256,1024]{1,0:T(8,128)(2,1)S(1)}, u32[]{:S(2)}) copy-start(bf16[256,1024]{1,0:T(8,128)(2,1)S(1)} %collective-permute-done.refs_2_) | copy-start | bytes 1572868
  72.5 1.0 copy-start.10
  73.5 40.3 %all-to-all-start.3 = ((bf16[32,16,1024]{2,1,0:T(8,128)(2,1)}), bf16[32,16,1024]{2,1,0:T(8,128)(2,1)S(1)}, u32[]{:S(2)}, u32[]{:S(2)}) async-start(bf16[32,16,1024]{2,1,0:T(8,128)(2,1)} %get-tuple-element.27), calls=%async_computation.3 | async-start | bytes 2097152 | tf_op jit(solution)/shard_map/all_to_all | solution.py:354
  84.1 29.7 %collective-permute-start.1 = (bf16[256,1024]{1,0:T(8,128)(2,1)S(1)}, bf16[256,1024]{1,0:T(8,128)(2,1)S(1)}, u32[]{:S(2)}, u32[]{:S(2)}) collective-permute-start(bf16[256,1024]{1,0:T(8,128)(2,1)S(1)} %collective-permute-done.refs_2_), channel_id=1, source_target_pairs={{0,8},{2,10},{4,12},{6,14},{8,16},{10,18},{12,20},{14,22},{16,24},... | collective-permute-start | bytes 1572872 | tf_op jit(solution)/shard_map/ppermute | solution.py:177
  113.8 44.2 %copy-start.1 = (bf16[256,1024]{1,0:T(8,128)(2,1)}, bf16[256,1024]{1,0:T(8,128)(2,1)S(1)}, u32[]{:S(2)}) copy-start(bf16[256,1024]{1,0:T(8,128)(2,1)S(1)} %collective-permute-done.1.refs_3_) | copy-start | bytes 1572868
  113.8 34.7 %copy-start.9 = (bf16[32,16,1024]{2,1,0:T(8,128)(2,1)}, bf16[32,16,1024]{2,1,0:T(8,128)(2,1)S(1)}, u32[]{:S(2)}) copy-start(bf16[32,16,1024]{2,1,0:T(8,128)(2,1)S(1)} %all-to-all-done.3.refs_0_) | copy-start | bytes 3145732
  113.8 34.7 %all-to-all-start.2 = ((bf16[32,16,1024]{2,1,0:T(8,128)(2,1)}), bf16[32,16,1024]{2,1,0:T(8,128)(2,1)}, u32[]{:S(2)}, u32[]{:S(2)}) async-start(bf16[32,16,1024]{2,1,0:T(8,128)(2,1)} %get-tuple-element.26), calls=%async_computation.2 | async-start | bytes 2097152 | tf_op jit(solution)/shard_map/all_to_all | solution.py:354
  148.5 105.7 %all-to-all-start.1 = ((bf16[32,16,1024]{2,1,0:T(8,128)(2,1)}), bf16[32,16,1024]{2,1,0:T(8,128)(2,1)}, u32[]{:S(2)}, u32[]{:S(2)}) async-start(bf16[32,16,1024]{2,1,0:T(8,128)(2,1)} %get-tuple-element.22), calls=%async_computation.1 | async-start | bytes 2097152 | tf_op jit(solution)/shard_map/all_to_all | solution.py:354
  154.4 25.6 %collective-permute-start.6 = (bf16[256,1024]{1,0:T(8,128)(2,1)S(1)}, bf16[256,1024]{1,0:T(8,128)(2,1)S(1)}, u32[]{:S(2)}, u32[]{:S(2)}) collective-permute-start(bf16[256,1024]{1,0:T(8,128)(2,1)S(1)} %collective-permute-done.refs_2_), channel_id=1, source_target_pairs={{0,6},{2,4},{4,2},{6,0},{8,14},{10,12},{12,10},{14,8},{16,22},{18,... | collective-permute-start | bytes 1572872 | tf_op jit(solution)/shard_map/ppermute | solution.py:191
  154.9 34.5 %collective-permute-start.4 = (bf16[256,1024]{1,0:T(8,128)(2,1)S(1)}, bf16[256,1024]{1,0:T(8,128)(2,1)S(1)}, u32[]{:S(2)}, u32[]{:S(2)}) collective-permute-start(bf16[256,1024]{1,0:T(8,128)(2,1)S(1)} %collective-permute-done.refs_2_), channel_id=1, source_target_pairs={{0,4},{2,6},{4,0},{6,2},{8,12},{10,14},{12,8},{14,10},{16,20},{18,... | collective-permute-start | bytes 1572872 | tf_op jit(solution)/shard_map/ppermute | solution.py:191
  156.4 34.7 %collective-permute-start.2 = (bf16[256,1024]{1,0:T(8,128)(2,1)S(1)}, bf16[256,1024]{1,0:T(8,128)(2,1)S(1)}, u32[]{:S(2)}, u32[]{:S(2)}) collective-permute-start(bf16[256,1024]{1,0:T(8,128)(2,1)S(1)} %collective-permute-done.refs_2_), channel_id=1, source_target_pairs={{0,2},{2,0},{4,6},{6,4},{8,10},{10,8},{12,14},{14,12},{16,18},{18,... | collective-permute-start | bytes 1572872 | tf_op jit(solution)/shard_map/ppermute | solution.py:191
  159.0 43.3 %collective-permute-start.3 = (bf16[256,1024]{1,0:T(8,128)(2,1)}, bf16[256,1024]{1,0:T(8,128)(2,1)S(1)}, u32[]{:S(2)}, u32[]{:S(2)}) collective-permute-start(bf16[256,1024]{1,0:T(8,128)(2,1)} %get-tuple-element.30), channel_id=1, source_target_pairs={{0,2},{2,0},{4,6},{6,4},{8,10},{10,8},{12,14},{14,12},{16,18},{18,... | collective-permute-start | bytes 1572872 | tf_op jit(solution)/shard_map/ppermute | solution.py:193
  159.6 53.7 %collective-permute-start.7 = (bf16[256,1024]{1,0:T(8,128)(2,1)}, bf16[256,1024]{1,0:T(8,128)(2,1)S(1)}, u32[]{:S(2)}, u32[]{:S(2)}) collective-permute-start(bf16[256,1024]{1,0:T(8,128)(2,1)} %get-tuple-element.29), channel_id=1, source_target_pairs={{0,6},{2,4},{4,2},{6,0},{8,14},{10,12},{12,10},{14,8},{16,22},{18,... | collective-permute-start | bytes 1572872 | tf_op jit(solution)/shard_map/ppermute | solution.py:193
  179.9 33.3 %copy-start.3 = (bf16[256,1024]{1,0:T(8,128)(2,1)}, bf16[256,1024]{1,0:T(8,128)(2,1)S(1)}, u32[]{:S(2)}) copy-start(bf16[256,1024]{1,0:T(8,128)(2,1)S(1)} %collective-permute-done.6.refs_8_) | copy-start | bytes 1572868
  179.9 33.3 %collective-permute-start.5 = (bf16[256,1024]{1,0:T(8,128)(2,1)}, bf16[256,1024]{1,0:T(8,128)(2,1)}, u32[]{:S(2)}, u32[]{:S(2)}) collective-permute-start(bf16[256,1024]{1,0:T(8,128)(2,1)} %get-tuple-element.29), channel_id=1, source_target_pairs={{0,4},{2,6},{4,0},{6,2},{8,12},{10,14},{12,8},{14,10},{16,20},{18,... | collective-permute-start | bytes 1572872 | tf_op jit(solution)/shard_map/ppermute | solution.py:193
  189.4 23.9 %copy-start.4 = (bf16[256,1024]{1,0:T(8,128)(2,1)}, bf16[256,1024]{1,0:T(8,128)(2,1)S(1)}, u32[]{:S(2)}) copy-start(bf16[256,1024]{1,0:T(8,128)(2,1)S(1)} %collective-permute-done.4.refs_6_) | copy-start | bytes 1572868
  191.1 22.2 %copy-start.5 = (bf16[256,1024]{1,0:T(8,128)(2,1)}, bf16[256,1024]{1,0:T(8,128)(2,1)S(1)}, u32[]{:S(2)}) copy-start(bf16[256,1024]{1,0:T(8,128)(2,1)S(1)} %collective-permute-done.2.refs_4_) | copy-start | bytes 1572868
  202.3 11.0 %copy-start.6 = (bf16[256,1024]{1,0:T(8,128)(2,1)}, bf16[256,1024]{1,0:T(8,128)(2,1)S(1)}, u32[]{:S(2)}) copy-start(bf16[256,1024]{1,0:T(8,128)(2,1)S(1)} %collective-permute-done.3.refs_5_) | copy-start | bytes 1572868
  (1 other events, 0.8 us)
where the time goes:
time: 269 us; the launch traced here: 268 us
  waiting for transfers between devices  150 us (56%)
  Pallas kernels  63 us (23%)
  starting transfers between devices  48.3 us (18%)
  local copies, waits for them, and re-layouts  3.44 us (1%)
    pallas_call x7, Pallas kernels, call(): pl.pallas_call(kernel, out_shape=outs, grid_spec=pltpu.PrefetchScalarGrid...  63 us
    ppermute x2, waiting for transfers between devices, forward(): lax.ppermute(x, 'ctx', [(s, s + plane) for s in range(shards - plane)])  56.7 us
    all_to_all x5, waiting for transfers between devices, exchange(): lax.all_to_all(sends, ('ctx', 'head'), split_axis=0, concat_axis=0, tiled...  43.2 us
    all_to_all x5, starting transfers between devices, exchange(): lax.all_to_all(sends, ('ctx', 'head'), split_axis=0, concat_axis=0, tiled...  38.7 us
    ppermute x3, waiting for transfers between devices, spread(): units.append(lax.ppermute(before, 'ctx', route))  28 us
    ppermute x3, waiting for transfers between devices, spread(): units.append(lax.ppermute(sent[bit], 'ctx', route))  22.2 us
  transfers between devices with their start and end apart: 13, of which 9 were waited for; matrix products, arithmetic and copies ran while one was open for 1% of the time, Pallas kernels for 17%

commit v1 on v0

--- a/solution.py
+++ b/solution.py
@@ -181,6 +181,7 @@
     units = [unit, before, oldest]
     places = [jnp.int32(SPAN), jnp.int32(plane), jnp.int32(0)]
     sent = {}
+    stages = [[1], [2], []]
     for mask in range(1, plane):
         partner = place ^ mask
         lower = place < partner
@@ -188,11 +189,13 @@
         if bit not in sent:
             sent[bit] = jnp.where(lower, unit, oldest)
         route = [(s, s ^ mask) for s in range(shards)]
+        stages[1].append(len(units))
         units.append(lax.ppermute(before, "ctx", route))
         places.append(plane - place + partner)
+        stages[2].append(len(units))
         units.append(lax.ppermute(sent[bit], "ctx", route))
         places.append(jnp.where(lower, 0, SPAN) - place + partner)
-    return units, jnp.stack(places).astype(jnp.int32)
+    return units, jnp.stack(places).astype(jnp.int32), stages
 
 
 def attend_kernel(chunk, docs, heads, slot_ref, lengths_ref, shard_ref, places_ref, *refs):
@@ -245,11 +248,13 @@
 
     lax.fori_loop(0, first_tile, unused, 0)
 
-    def step(index, masked, last):
-        landed(index)
-        tile_keys = keys[index]
-        tile_values = values[index]
-        extended = jnp.concatenate([tile_values, jnp.ones((tile, HD), tile_values.dtype)], axis=1)
+    def step(index, count, masked, last):
+        for other in range(count):
+            landed(index + other)
+        span = count * tile
+        tile_keys = keys[pl.ds(index, count)].reshape(span, HD)
+        tile_values = values[pl.ds(index, count)].reshape(span, HD)
+        extended = jnp.concatenate([tile_values, jnp.ones((span, HD), tile_values.dtype)], axis=1)
         turned = extended.T[: HD + 16]
         if masked:
             key_rows = window_start + index * tile + lax.broadcasted_iota(jnp.int32, (tile, rows), 0)
@@ -288,14 +293,20 @@
 
     @pl.when(first_tile < diagonal)
     def _():
-        step(first_tile, True, False)
+        step(first_tile, 1, True, False)
+
+    between = jnp.maximum(diagonal - first_tile - 1, 0)
+
+    @pl.when(between % 2 == 1)
+    def _():
+        step(first_tile + 1, 1, False, False)
 
     def middle(index, carry):
-        step(index, False, False)
+        step(first_tile + 1 + between % 2 + 2 * index, 2, False, False)
         return carry
 
-    lax.fori_loop(first_tile + 1, diagonal, middle, 0)
-    step(diagonal, True, True)
+    lax.fori_loop(0, between // 2, middle, 0)
+    step(diagonal, 1, True, True)
 
 
 def attend(arrived, units, places, slots, doc_lengths, shard, chunk, chunks, result):
@@ -361,10 +372,12 @@
     sources = inverse // per_loader
     unit = pick_unit(pair, sources)
     sends[0], unit = lax.optimization_barrier((sends[0], unit))
-    units, unit_places = spread(unit, shard)
-    for chunk, stage in ((1, 1), (2, 2), (3, 2)):
-        if chunk < chunks:
-            sends[chunk], units[stage] = lax.optimization_barrier((sends[chunk], units[stage]))
+    units, unit_places, stages = spread(unit, shard)
+    for chunk, stage in enumerate(stages[: chunks - 1]):
+        held = [units[at] for at in stage]
+        held, sends[chunk + 1] = lax.optimization_barrier((held, sends[chunk + 1]))
+        for at, value in zip(stage, held):
+            units[at] = value
     arrived = [exchange(send) for send in sends]
     result = None
     for chunk in range(chunks):

time: 269 us -> 220 us (0.82)
  the two profiles are of different devices: /device:TPU:30 before, /device:TPU:14 now
where the time goes in v1:
time: 220 us; the launch traced here: 218 us
  waiting for transfers between devices  112 us (51%)
  Pallas kernels  57.9 us (26%)
  starting transfers between devices  43.1 us (20%)
  local copies, waits for them, and re-layouts  3.68 us (2%)
    pallas_call x7, Pallas kernels, call(): pl.pallas_call(kernel, out_shape=outs, grid_spec=pltpu.PrefetchScalarGrid...  57.9 us
    ppermute x3, waiting for transfers between devices, spread(): units.append(lax.ppermute(sent[bit], 'ctx', route))  31.6 us
    ppermute x2, waiting for transfers between devices, forward(): lax.ppermute(x, 'ctx', [(s, s + plane) for s in range(shards - plane)])  31 us
    ppermute x3, waiting for transfers between devices, spread(): units.append(lax.ppermute(before, 'ctx', route))  29.8 us
    all_to_all x5, starting transfers between devices, exchange(): lax.all_to_all(sends, ('ctx', 'head'), split_axis=0, concat_axis=0, tiled...  29.2 us
    all_to_all x5, waiting for transfers between devices, exchange(): lax.all_to_all(sends, ('ctx', 'head'), split_axis=0, concat_axis=0, tiled...  19.2 us
    ppermute x2, starting transfers between devices, forward(): lax.ppermute(x, 'ctx', [(s, s + plane) for s in range(shards - plane)])  6.79 us
  transfers between devices with their start and end apart: 13, of which 7 were waited for; matrix products, arithmetic and copies ran while one was open for 1% of the time, Pallas kernels for 18%

profile of v1, /device:TPU:14, one launch (start us, length us, event | category | flops | bytes accessed | tf_op | source)
XLA Modules:
  0.0 218.3 jit_solution(14683867379647905713)
XLA Ops:
  0.7 2.8 %pack_pair.1 = bf16[32,16,1024]{2,1,0:T(8,128)(2,1)} custom-call(s32[256]{0:T(256)} %place_ref.3, s32[2]{0:T(128)} %pad_add_fusion.loader_ref, bf16[8,16,1024]{2,1,0:T(8,128)(2,1)} %bitcast.19, bf16[8,16,1024]{2,1,0:T(8,128)(2,1)} %bitcast.20), custom_call_target="tpu_custom_call" | custom-call | bytes 1048576 | tf_op jit(solution)/shard_map/pack_pair/pallas_call | solution.py:63
  3.5 6.0 %all-to-all-start = ((bf16[32,16,1024]{2,1,0:T(8,128)(2,1)}), bf16[32,16,1024]{2,1,0:T(8,128)(2,1)S(1)}, u32[]{:S(2)}, u32[]{:S(2)}) async-start(bf16[32,16,1024]{2,1,0:T(8,128)(2,1)} %pack_pair.1), calls=%async_computation | async-start | bytes 2097152 | tf_op jit(solution)/shard_map/all_to_all | solution.py:365
  9.5 4.1 %pack_query.1 = (bf16[32,16,1024]{2,1,0:T(8,128)(2,1)}, bf16[32,16,1024]{2,1,0:T(8,128)(2,1)}, bf16[32,16,1024]{2,1,0:T(8,128)(2,1)}, bf16[32,16,1024]{2,1,0:T(8,128)(2,1)}) custom-call(s32[256]{0:T(256)} %place_ref.3, s32[2]{0:T(128)} %pad_add_fusion.loader_ref, bf16[8,16,8192]{2,1,0:T(8,128)(2,1)} %bitcast.18), custom_call_target="tpu_custom_call" | custom-call | bytes 4194304 | tf_op jit(solution)/shard_map/pack_query/pallas_call | solution.py:63
  14.4 19.2 %all-to-all-done.blocks = bf16[32,16,1024]{2,1,0:T(8,128)(2,1)S(1)} async-done(((bf16[32,16,1024]{2,1,0:T(8,128)(2,1)}), bf16[32,16,1024]{2,1,0:T(8,128)(2,1)S(1)}, u32[]{:S(2)}, u32[]{:S(2)}) %all-to-all-start) | async-done | bytes 1048608 | tf_op jit(solution)/shard_map/all_to_all | solution.py:365
  34.6 2.6 %pick_unit.1 = bf16[16,16,1024]{2,1,0:T(8,128)(2,1)} custom-call(s32[16]{0:T(128)} %and_select_fusion.rows_ref.slot_ref, bf16[32,16,1024]{2,1,0:T(8,128)(2,1)} %copy-done.9), custom_call_target="tpu_custom_call" | custom-call | bytes 1048576 | tf_op jit(solution)/shard_map/pick_unit/pallas_call | solution.py:63
  37.2 5.8 %all-to-all-start.4 = ((bf16[32,16,1024]{2,1,0:T(8,128)(2,1)}), bf16[32,16,1024]{2,1,0:T(8,128)(2,1)S(1)}, u32[]{:S(2)}, u32[]{:S(2)}) async-start(bf16[32,16,1024]{2,1,0:T(8,128)(2,1)} %get-tuple-element.38), calls=%async_computation.4 | async-start | bytes 2097152 | tf_op jit(solution)/shard_map/all_to_all | solution.py:365
  42.9 3.4 %collective-permute-start = (bf16[256,1024]{1,0:T(8,128)(2,1)S(1)}, bf16[256,1024]{1,0:T(8,128)(2,1)S(1)}, u32[]{:S(2)}, u32[]{:S(2)}) collective-permute-start(bf16[256,1024]{1,0:T(8,128)(2,1)S(1)} %bitcast.16), channel_id=1, source_target_pairs={{0,8},{2,10},{4,12},{6,14},{8,16},{10,18},{12,20},{14,22},{16,24},... | collective-permute-start | bytes 1572872 | tf_op jit(solution)/shard_map/ppermute | solution.py:177
  46.4 31.0 %collective-permute-done.refs_2_ = bf16[256,1024]{1,0:T(8,128)(2,1)S(1)} collective-permute-done((bf16[256,1024]{1,0:T(8,128)(2,1)S(1)}, bf16[256,1024]{1,0:T(8,128)(2,1)S(1)}, u32[]{:S(2)}, u32[]{:S(2)}) %collective-permute-start) | collective-permute-done | bytes 524320 | tf_op jit(solution)/shard_map/ppermute | solution.py:177
  78.3 5.9 %all-to-all-start.3 = ((bf16[32,16,1024]{2,1,0:T(8,128)(2,1)}), bf16[32,16,1024]{2,1,0:T(8,128)(2,1)}, u32[]{:S(2)}, u32[]{:S(2)}) async-start(bf16[32,16,1024]{2,1,0:T(8,128)(2,1)} %get-tuple-element.37), calls=%async_computation.3 | async-start | bytes 2097152 | tf_op jit(solution)/shard_map/all_to_all | solution.py:365
  84.9 1.5 collective-permute-start.6
  86.3 1.5 collective-permute-start.5
  87.8 3.4 %collective-permute-start.1 = (bf16[256,1024]{1,0:T(8,128)(2,1)S(1)}, bf16[256,1024]{1,0:T(8,128)(2,1)S(1)}, u32[]{:S(2)}, u32[]{:S(2)}) collective-permute-start(bf16[256,1024]{1,0:T(8,128)(2,1)S(1)} %collective-permute-done.refs_2_), channel_id=1, source_target_pairs={{0,8},{2,10},{4,12},{6,14},{8,16},{10,18},{12,20},{14,22},{16,24},... | collective-permute-start | bytes 1572872 | tf_op jit(solution)/shard_map/ppermute | solution.py:177
  91.2 18.5 %collective-permute-done.7.refs_8_ = bf16[256,1024]{1,0:T(8,128)(2,1)S(1)} collective-permute-done((bf16[256,1024]{1,0:T(8,128)(2,1)S(1)}, bf16[256,1024]{1,0:T(8,128)(2,1)S(1)}, u32[]{:S(2)}, u32[]{:S(2)}) %collective-permute-start.7) | collective-permute-done | bytes 524320 | tf_op jit(solution)/shard_map/ppermute | solution.py:193
  109.7 9.9 %collective-permute-done.6.refs_6_ = bf16[256,1024]{1,0:T(8,128)(2,1)S(1)} collective-permute-done((bf16[256,1024]{1,0:T(8,128)(2,1)S(1)}, bf16[256,1024]{1,0:T(8,128)(2,1)S(1)}, u32[]{:S(2)}, u32[]{:S(2)}) %collective-permute-start.6) | collective-permute-done | bytes 524320 | tf_op jit(solution)/shard_map/ppermute | solution.py:193
  119.5 1.5 collective-permute-done.5.refs_4_
  121.1 5.8 %all-to-all-start.2 = ((bf16[32,16,1024]{2,1,0:T(8,128)(2,1)}), bf16[32,16,1024]{2,1,0:T(8,128)(2,1)}, u32[]{:S(2)}, u32[]{:S(2)}) async-start(bf16[32,16,1024]{2,1,0:T(8,128)(2,1)} %get-tuple-element.36), calls=%async_computation.2 | async-start | bytes 2097152 | tf_op jit(solution)/shard_map/all_to_all | solution.py:365
  129.1 1.5 collective-permute-start.3
  130.5 20.8 %collective-permute-done.2.refs_5_ = bf16[256,1024]{1,0:T(8,128)(2,1)S(1)} collective-permute-done((bf16[256,1024]{1,0:T(8,128)(2,1)S(1)}, bf16[256,1024]{1,0:T(8,128)(2,1)S(1)}, u32[]{:S(2)}, u32[]{:S(2)}) %collective-permute-start.2) | collective-permute-done | bytes 524320 | tf_op jit(solution)/shard_map/ppermute | solution.py:196
  151.4 10.8 %collective-permute-done.4.refs_9_ = bf16[256,1024]{1,0:T(8,128)(2,1)S(1)} collective-permute-done((bf16[256,1024]{1,0:T(8,128)(2,1)S(1)}, bf16[256,1024]{1,0:T(8,128)(2,1)S(1)}, u32[]{:S(2)}, u32[]{:S(2)}) %collective-permute-start.4) | collective-permute-done | bytes 524320 | tf_op jit(solution)/shard_map/ppermute | solution.py:196
  162.1 5.8 %all-to-all-start.1 = ((bf16[32,16,1024]{2,1,0:T(8,128)(2,1)}), bf16[32,16,1024]{2,1,0:T(8,128)(2,1)S(1)}, u32[]{:S(2)}, u32[]{:S(2)}) async-start(bf16[32,16,1024]{2,1,0:T(8,128)(2,1)} %get-tuple-element.25), calls=%async_computation.1 | async-start | bytes 2097152 | tf_op jit(solution)/shard_map/all_to_all | solution.py:365
  168.7 12.0 %attend0.1.refs_10_ = bf16[256,4096]{1,0:T(8,128)(2,1)} custom-call(s32[16]{0:T(128)} %and_select_fusion.rows_ref.slot_ref, s32[4]{0:T(128)} %lengths_ref.7, s32[1]{0:T(128)} %bitcast.shard_ref, s32[9]{0:T(128)} %stack.35.places_ref, bf16[32,16,1024]{2,1,0:T(8,128)(2,1)} %copy-done.11, bf16[256,1024]{1,0:T(8,128)(2,1)} %bitcast.12, ...), custom_call_target="tpu_custom_call" | custom-call | flops 2415919104 | bytes 2228224 | tf_op jit(solution)/shard_map/attend0/pallas_call | solution.py:63
  180.7 12.2 %attend1.1.refs_10_ = bf16[256,4096]{1,0:T(8,128)(2,1)} custom-call(s32[16]{0:T(128)} %and_select_fusion.rows_ref.slot_ref, s32[4]{0:T(128)} %lengths_ref.7, s32[1]{0:T(128)} %bitcast.shard_ref, s32[9]{0:T(128)} %stack.35.places_ref, bf16[32,16,1024]{2,1,0:T(8,128)(2,1)} %all-to-all-done.3.refs_0_, ...), custom_call_target="tpu_custom_call", output_to_operand_aliasing={{}: (14, {})} | custom-call | flops 2415919104 | bytes 2228224 | tf_op jit(solution)/shard_map/attend1/pallas_call | solution.py:63
  192.9 12.0 %attend2.1.refs_10_ = bf16[256,4096]{1,0:T(8,128)(2,1)} custom-call(s32[16]{0:T(128)} %and_select_fusion.rows_ref.slot_ref, s32[4]{0:T(128)} %lengths_ref.7, s32[1]{0:T(128)} %bitcast.shard_ref, s32[9]{0:T(128)} %stack.35.places_ref, bf16[32,16,1024]{2,1,0:T(8,128)(2,1)} %all-to-all-done.2.refs_0_, ...), custom_call_target="tpu_custom_call", output_to_operand_aliasing={{}: (14, {})} | custom-call | flops 2415919104 | bytes 2228224 | tf_op jit(solution)/shard_map/attend2/pallas_call | solution.py:63
  205.9 12.2 %attend3.1 = bf16[256,4096]{1,0:T(8,128)(2,1)} custom-call(s32[16]{0:T(128)} %and_select_fusion.rows_ref.slot_ref, s32[4]{0:T(128)} %lengths_ref.7, s32[1]{0:T(128)} %bitcast.shard_ref, s32[9]{0:T(128)} %stack.35.places_ref, bf16[32,16,1024]{2,1,0:T(8,128)(2,1)} %copy-done.10, bf16[256,1024]{1,0:T(8,128)(2,1)} %bitcast.15, ...), custom_call_target="tpu_custom_call", output_to_operand_aliasing={{}: (14, {})} | custom-call | flops 2415919104 | bytes 2228224 | tf_op jit(solution)/shard_map/attend3/pallas_call | solution.py:63
  (41 shorter events, 7.9 us)
Async XLA Ops:
  3.5 10.1 %copy-start.12 = (s32[256]{0:T(256)S(1)}, s32[256]{0:T(256)}, u32[]{:S(2)}) copy-start(s32[256]{0:T(256)} %place_ref.3) | copy-start | bytes 3076
  3.5 30.1 %all-to-all-start = ((bf16[32,16,1024]{2,1,0:T(8,128)(2,1)}), bf16[32,16,1024]{2,1,0:T(8,128)(2,1)S(1)}, u32[]{:S(2)}, u32[]{:S(2)}) async-start(bf16[32,16,1024]{2,1,0:T(8,128)(2,1)} %pack_pair.1), calls=%async_computation | async-start | bytes 2097152 | tf_op jit(solution)/shard_map/all_to_all | solution.py:365
  37.2 5.8 %copy-start = (bf16[16,16,1024]{2,1,0:T(8,128)(2,1)S(1)}, bf16[16,16,1024]{2,1,0:T(8,128)(2,1)}, u32[]{:S(2)}) copy-start(bf16[16,16,1024]{2,1,0:T(8,128)(2,1)} %pick_unit.1) | copy-start | bytes 1572868
  37.2 40.2 %all-to-all-start.4 = ((bf16[32,16,1024]{2,1,0:T(8,128)(2,1)}), bf16[32,16,1024]{2,1,0:T(8,128)(2,1)S(1)}, u32[]{:S(2)}, u32[]{:S(2)}) async-start(bf16[32,16,1024]{2,1,0:T(8,128)(2,1)} %get-tuple-element.38), calls=%async_computation.4 | async-start | bytes 2097152 | tf_op jit(solution)/shard_map/all_to_all | solution.py:365
  42.9 34.4 %collective-permute-start = (bf16[256,1024]{1,0:T(8,128)(2,1)S(1)}, bf16[256,1024]{1,0:T(8,128)(2,1)S(1)}, u32[]{:S(2)}, u32[]{:S(2)}) collective-permute-start(bf16[256,1024]{1,0:T(8,128)(2,1)S(1)} %bitcast.16), channel_id=1, source_target_pairs={{0,8},{2,10},{4,12},{6,14},{8,16},{10,18},{12,20},{14,22},{16,24},... | collective-permute-start | bytes 1572872 | tf_op jit(solution)/shard_map/ppermute | solution.py:177
  77.3 43.7 %copy-start.2 = (bf16[256,1024]{1,0:T(8,128)(2,1)}, bf16[256,1024]{1,0:T(8,128)(2,1)S(1)}, u32[]{:S(2)}) copy-start(bf16[256,1024]{1,0:T(8,128)(2,1)S(1)} %collective-permute-done.refs_2_) | copy-start | bytes 1572868
  77.3 1.0 copy-start.11
  78.3 42.7 %all-to-all-start.3 = ((bf16[32,16,1024]{2,1,0:T(8,128)(2,1)}), bf16[32,16,1024]{2,1,0:T(8,128)(2,1)}, u32[]{:S(2)}, u32[]{:S(2)}) async-start(bf16[32,16,1024]{2,1,0:T(8,128)(2,1)} %get-tuple-element.37), calls=%async_computation.3 | async-start | bytes 2097152 | tf_op jit(solution)/shard_map/all_to_all | solution.py:365
  84.2 25.4 %collective-permute-start.7 = (bf16[256,1024]{1,0:T(8,128)(2,1)S(1)}, bf16[256,1024]{1,0:T(8,128)(2,1)S(1)}, u32[]{:S(2)}, u32[]{:S(2)}) collective-permute-start(bf16[256,1024]{1,0:T(8,128)(2,1)S(1)} %collective-permute-done.refs_2_), channel_id=1, source_target_pairs={{0,6},{2,4},{4,2},{6,0},{8,14},{10,12},{12,10},{14,8},{16,22},{18,... | collective-permute-start | bytes 1572872 | tf_op jit(solution)/shard_map/ppermute | solution.py:193
  84.9 34.7 %collective-permute-start.6 = (bf16[256,1024]{1,0:T(8,128)(2,1)S(1)}, bf16[256,1024]{1,0:T(8,128)(2,1)S(1)}, u32[]{:S(2)}, u32[]{:S(2)}) collective-permute-start(bf16[256,1024]{1,0:T(8,128)(2,1)S(1)} %collective-permute-done.refs_2_), channel_id=1, source_target_pairs={{0,4},{2,6},{4,0},{6,2},{8,12},{10,14},{12,8},{14,10},{16,20},{18,... | collective-permute-start | bytes 1572872 | tf_op jit(solution)/shard_map/ppermute | solution.py:193
  86.3 34.7 %collective-permute-start.5 = (bf16[256,1024]{1,0:T(8,128)(2,1)S(1)}, bf16[256,1024]{1,0:T(8,128)(2,1)S(1)}, u32[]{:S(2)}, u32[]{:S(2)}) collective-permute-start(bf16[256,1024]{1,0:T(8,128)(2,1)S(1)} %collective-permute-done.refs_2_), channel_id=1, source_target_pairs={{0,2},{2,0},{4,6},{6,4},{8,10},{10,8},{12,14},{14,12},{16,18},{18,... | collective-permute-start | bytes 1572872 | tf_op jit(solution)/shard_map/ppermute | solution.py:193
  87.8 33.2 %collective-permute-start.1 = (bf16[256,1024]{1,0:T(8,128)(2,1)S(1)}, bf16[256,1024]{1,0:T(8,128)(2,1)S(1)}, u32[]{:S(2)}, u32[]{:S(2)}) collective-permute-start(bf16[256,1024]{1,0:T(8,128)(2,1)S(1)} %collective-permute-done.refs_2_), channel_id=1, source_target_pairs={{0,8},{2,10},{4,12},{6,14},{8,16},{10,18},{12,20},{14,22},{16,24},... | collective-permute-start | bytes 1572872 | tf_op jit(solution)/shard_map/ppermute | solution.py:177
  109.7 17.3 %copy-start.3 = (bf16[256,1024]{1,0:T(8,128)(2,1)}, bf16[256,1024]{1,0:T(8,128)(2,1)S(1)}, u32[]{:S(2)}) copy-start(bf16[256,1024]{1,0:T(8,128)(2,1)S(1)} %collective-permute-done.7.refs_8_) | copy-start | bytes 1572868
  119.5 7.4 %copy-start.4 = (bf16[256,1024]{1,0:T(8,128)(2,1)}, bf16[256,1024]{1,0:T(8,128)(2,1)S(1)}, u32[]{:S(2)}) copy-start(bf16[256,1024]{1,0:T(8,128)(2,1)S(1)} %collective-permute-done.6.refs_6_) | copy-start | bytes 1572868
  121.0 5.9 %copy-start.5 = (bf16[256,1024]{1,0:T(8,128)(2,1)}, bf16[256,1024]{1,0:T(8,128)(2,1)S(1)}, u32[]{:S(2)}) copy-start(bf16[256,1024]{1,0:T(8,128)(2,1)S(1)} %collective-permute-done.5.refs_4_) | copy-start | bytes 1572868
  121.0 5.9 %copy-start.1 = (bf16[256,1024]{1,0:T(8,128)(2,1)}, bf16[256,1024]{1,0:T(8,128)(2,1)S(1)}, u32[]{:S(2)}) copy-start(bf16[256,1024]{1,0:T(8,128)(2,1)S(1)} %collective-permute-done.1.refs_3_) | copy-start | bytes 1572868
  121.1 41.1 %all-to-all-start.2 = ((bf16[32,16,1024]{2,1,0:T(8,128)(2,1)}), bf16[32,16,1024]{2,1,0:T(8,128)(2,1)}, u32[]{:S(2)}, u32[]{:S(2)}) async-start(bf16[32,16,1024]{2,1,0:T(8,128)(2,1)} %get-tuple-element.36), calls=%async_computation.2 | async-start | bytes 2097152 | tf_op jit(solution)/shard_map/all_to_all | solution.py:365
  127.0 24.4 %collective-permute-start.2 = (bf16[256,1024]{1,0:T(8,128)(2,1)S(1)}, bf16[256,1024]{1,0:T(8,128)(2,1)S(1)}, u32[]{:S(2)}, u32[]{:S(2)}) collective-permute-start(bf16[256,1024]{1,0:T(8,128)(2,1)S(1)} %get-tuple-element.40), channel_id=1, source_target_pairs={{0,2},{2,0},{4,6},{6,4},{8,10},{10,8},{12,14},{14,12},{16,18},{18,... | collective-permute-start | bytes 1572872 | tf_op jit(solution)/shard_map/ppermute | solution.py:196
  127.6 34.5 %collective-permute-start.4 = (bf16[256,1024]{1,0:T(8,128)(2,1)S(1)}, bf16[256,1024]{1,0:T(8,128)(2,1)S(1)}, u32[]{:S(2)}, u32[]{:S(2)}) collective-permute-start(bf16[256,1024]{1,0:T(8,128)(2,1)S(1)} %get-tuple-element.39), channel_id=1, source_target_pairs={{0,6},{2,4},{4,2},{6,0},{8,14},{10,12},{12,10},{14,8},{16,22},{18,... | collective-permute-start | bytes 1572872 | tf_op jit(solution)/shard_map/ppermute | solution.py:196
  129.1 33.1 %collective-permute-start.3 = (bf16[256,1024]{1,0:T(8,128)(2,1)S(1)}, bf16[256,1024]{1,0:T(8,128)(2,1)S(1)}, u32[]{:S(2)}, u32[]{:S(2)}) collective-permute-start(bf16[256,1024]{1,0:T(8,128)(2,1)S(1)} %get-tuple-element.39), channel_id=1, source_target_pairs={{0,4},{2,6},{4,0},{6,2},{8,12},{10,14},{12,8},{14,10},{16,20},{18,... | collective-permute-start | bytes 1572872 | tf_op jit(solution)/shard_map/ppermute | solution.py:196
  151.4 17.3 %copy-start.6 = (bf16[256,1024]{1,0:T(8,128)(2,1)}, bf16[256,1024]{1,0:T(8,128)(2,1)S(1)}, u32[]{:S(2)}) copy-start(bf16[256,1024]{1,0:T(8,128)(2,1)S(1)} %collective-permute-done.2.refs_5_) | copy-start | bytes 1572868
  162.1 6.5 %copy-start.7 = (bf16[256,1024]{1,0:T(8,128)(2,1)}, bf16[256,1024]{1,0:T(8,128)(2,1)S(1)}, u32[]{:S(2)}) copy-start(bf16[256,1024]{1,0:T(8,128)(2,1)S(1)} %collective-permute-done.4.refs_9_) | copy-start | bytes 1572868
  162.1 6.5 %copy-start.8 = (bf16[256,1024]{1,0:T(8,128)(2,1)}, bf16[256,1024]{1,0:T(8,128)(2,1)S(1)}, u32[]{:S(2)}) copy-start(bf16[256,1024]{1,0:T(8,128)(2,1)S(1)} %collective-permute-done.3.refs_7_) | copy-start | bytes 1572868
  162.1 42.7 %all-to-all-start.1 = ((bf16[32,16,1024]{2,1,0:T(8,128)(2,1)}), bf16[32,16,1024]{2,1,0:T(8,128)(2,1)S(1)}, u32[]{:S(2)}, u32[]{:S(2)}) async-start(bf16[32,16,1024]{2,1,0:T(8,128)(2,1)} %get-tuple-element.25), calls=%async_computation.1 | async-start | bytes 2097152 | tf_op jit(solution)/shard_map/all_to_all | solution.py:365
  (2 other events, 2.0 us)
